TPU v7x, 256 devices: a whole 4x4x8 slice. The times are simulated.
256 devices in a mesh: rack: 4 (over x), outer: 16 (over z, core), tp: 4 (over y).
Axes of the slice: x: 4, y: 4, z: 8, core: 2. Of those that a mesh axis runs over, the one named last changes fastest.
Arguments:
- context: bfloat16 [65536, 6144], P(('rack', 'outer'), 'tp'), may hold values from -0.8 to 0.8
- cotangent: bfloat16 [65536, 3072], P(('rack', 'outer')), may hold values from -40 to 40
Outputs:
- merged_grad: bfloat16 [3072, 6144], P(('rack', 'outer'), 'tp')
All inputs are finite; a program needn't handle non-finite values.
Results may differ from a plain program's by a relative error of at most 0.015.
Values may be sent and summed in bfloat16 or wider, within the bound.
A program may use at most 64 MiB of HBM per device.

v0:
```python
import jax
import jax.numpy as jnp
from jax import lax
from jax.sharding import PartitionSpec as P

EPS = 1e-06


def from_partner(array, axis, distance):
    return lax.ppermute(array, axis, [(i, i ^ 1 << distance) for i in range(lax.axis_size(axis))])


def mix_pair(first, second, ab, aa, bb):
    mixed = (1.0 - ab / (2.0 * (aa + EPS))) * first + (1.0 - ab / (2.0 * (bb + EPS))) * second
    return mixed.astype(jnp.bfloat16)


def shards(context, cotangent):
    rows_here = cotangent.shape[1] // lax.axis_size("rack")
    summed = lax.psum_scatter(
        lax.dot_general(
            cotangent, context, (((0,), (0,)), ((), ())), preferred_element_type=jnp.float32
        ).astype(jnp.bfloat16),
        "rack",
        scatter_dimension=0,
        tiled=True,
    )
    outer_n = lax.axis_size("outer")
    level_count = outer_n.bit_length() - 1
    block_rows = rows_here // outer_n
    position = lax.axis_index("outer")
    current = summed
    for level in range(level_count):
        other = from_partner(current, "outer", level)
        first = current.astype(jnp.float32)
        second = other.astype(jnp.float32)
        ab, aa, bb = lax.psum(
            (jnp.sum(first * second), jnp.sum(first * first), jnp.sum(second * second)),
            ("rack", "tp"),
        )
        current = mix_pair(first, second, ab, aa, bb)
    return lax.dynamic_slice_in_dim(current, position * block_rows, block_rows, 0)


def solution(mesh):
    return jax.shard_map(
        shards,
        mesh=mesh,
        in_specs=(P(("rack", "outer"), "tp"), P(("rack", "outer"), None)),
        out_specs=P(("rack", "outer"), "tp"),
        check_vma=False,
    )
```

profile of v0, /device:TPU:8, one launch (start us, length us, event | category | flops | bytes accessed | tf_op | source)
XLA Modules:
  0.0 557.5 jit_solution(4686028644098582616)
XLA Ops:
  6.5 1.9 copy-done
  8.4 14.9 %convolution_convert_fusion = bf16[3072,1536]{1,0:T(8,128)(2,1)} fusion(bf16[1024,3072]{1,0:T(8,128)(2,1)} %param.3, bf16[1024,1536]{1,0:T(8,128)(2,1)S(1)} %copy-done), kind=kOutput, calls=%fused_computation | convolution fusion | flops 9668395008 | bytes 18874368 | tf_op jit(solution)/shard_map/dot_general | solution.py:21
  23.4 94.5 %reduce-scatter.2.cloned.1.call-done = bf16[768,1536]{1,0:T(8,128)(2,1)} async-done(((bf16[3072,1536]{1,0:T(8,128)(2,1)}), bf16[768,1536]{1,0:T(8,128)(2,1)}) %reduce-scatter.2.cloned.1.call-update) | async-done | bytes 2359312 | tf_op jit(solution)/shard_map/reduce_scatter | solution.py:20
  117.9 4.7 collective-permute-done
  122.6 1.4 copy-done.4
  124.1 3.8 fusion
  127.9 36.7 %all-reduce.3 = (f32[]{:T(128)}, f32[]{:T(128)}, f32[]{:T(128)}) all-reduce(f32[]{:T(128)} %get-tuple-element.15, f32[]{:T(128)} %get-tuple-element.16, f32[]{:T(128)} %get-tuple-element.14), channel_id=1, replica_groups=mesh['rack'=4,'outer'=16,'tp'=4] {'rack','tp'}, use_global_device_ids=true, to_apply=%region_2.0 | all-reduce | flops 3 | bytes 24 | tf_op jit(solution)/shard_map/psum | solution.py:37
  167.1 3.2 fusion.2
  170.4 1.6 collective-permute-start.1
  172.0 44.5 %collective-permute-done.1 = bf16[768,1536]{1,0:T(8,128)(2,1)S(1)} collective-permute-done((bf16[768,1536]{1,0:T(8,128)(2,1)S(1)}, bf16[768,1536]{1,0:T(8,128)(2,1)S(1)}, u32[]{:S(2)}, u32[]{:S(2)}) %collective-permute-start.1) | collective-permute-done | bytes 2359328 | tf_op jit(solution)/shard_map/ppermute | solution.py:10
  216.6 2.1 fusion.5
  218.6 39.2 %all-reduce.2 = (f32[]{:T(128)}, f32[]{:T(128)}, f32[]{:T(128)}) all-reduce(f32[]{:T(128)} %get-tuple-element.12, f32[]{:T(128)} %get-tuple-element.13, f32[]{:T(128)} %get-tuple-element.11), channel_id=1, replica_groups=mesh['rack'=4,'outer'=16,'tp'=4] {'rack','tp'}, use_global_device_ids=true, to_apply=%region_8.0 | all-reduce | flops 3 | bytes 24 | tf_op jit(solution)/shard_map/psum | solution.py:37
  260.3 3.2 fusion.7
  263.6 2.6 collective-permute-start.2
  266.2 86.8 %collective-permute-done.2 = bf16[768,1536]{1,0:T(8,128)(2,1)S(1)} collective-permute-done((bf16[768,1536]{1,0:T(8,128)(2,1)S(1)}, bf16[768,1536]{1,0:T(8,128)(2,1)S(1)}, u32[]{:S(2)}, u32[]{:S(2)}) %collective-permute-start.2) | collective-permute-done | bytes 2359328 | tf_op jit(solution)/shard_map/ppermute | solution.py:10
  353.0 2.0 fusion.10
  355.1 36.7 %all-reduce.1 = (f32[]{:T(128)}, f32[]{:T(128)}, f32[]{:T(128)}) all-reduce(f32[]{:T(128)} %get-tuple-element.9, f32[]{:T(128)} %get-tuple-element.10, f32[]{:T(128)} %get-tuple-element.8), channel_id=1, replica_groups=mesh['rack'=4,'outer'=16,'tp'=4] {'rack','tp'}, use_global_device_ids=true, to_apply=%region_14.0 | all-reduce | flops 3 | bytes 24 | tf_op jit(solution)/shard_map/psum | solution.py:37
  394.3 6.2 %fusion.17 = (f32[768,1536]{1,0:T(8,128)}, bf16[768,1536]{1,0:T(8,128)(2,1)}) fusion(bf16[768,1536]{1,0:T(8,128)(2,1)} %copy-done.3, f32[]{:T(128)S(6)} %sub.29, bf16[768,1536]{1,0:T(8,128)(2,1)} %copy-done.1, f32[]{:T(128)S(6)} %sub.28), kind=kLoop, calls=%fused_computation.38 | loop fusion | flops 8257536 | bytes 11796488 | tf_op jit(solution)/shard_map/convert_element_type | solution.py:35
  400.5 5.7 %collective-permute-start.3 = (bf16[768,1536]{1,0:T(8,128)(2,1)}, bf16[768,1536]{1,0:T(8,128)(2,1)}, u32[]{:S(2)}, u32[]{:S(2)}) collective-permute-start(bf16[768,1536]{1,0:T(8,128)(2,1)} %get-tuple-element.30), channel_id=1, source_target_pairs={{0,32},{4,36},{8,40},{12,44},{16,48},{20,52},{24,56},{28,60},{32,0... | collective-permute-start | bytes 7077896 | tf_op jit(solution)/shard_map/ppermute | solution.py:10
  406.2 95.6 %collective-permute-done.3 = bf16[768,1536]{1,0:T(8,128)(2,1)} collective-permute-done((bf16[768,1536]{1,0:T(8,128)(2,1)}, bf16[768,1536]{1,0:T(8,128)(2,1)}, u32[]{:S(2)}, u32[]{:S(2)}) %collective-permute-start.3) | collective-permute-done | bytes 2359328 | tf_op jit(solution)/shard_map/ppermute | solution.py:10
  501.8 4.2 multiply_reduce_fusion.1
  506.1 38.1 %all-reduce = (f32[]{:T(128)}, f32[]{:T(128)}, f32[]{:T(128)}) all-reduce(f32[]{:T(128)} %get-tuple-element.6, f32[]{:T(128)} %get-tuple-element.7, f32[]{:T(128)} %get-tuple-element.5), channel_id=1, replica_groups=mesh['rack'=4,'outer'=16,'tp'=4] {'rack','tp'}, use_global_device_ids=true, to_apply=%region_20.0 | all-reduce | flops 3 | bytes 24 | tf_op jit(solution)/shard_map/psum | solution.py:37
  546.7 2.3 convert_element_type.50
  549.0 1.7 fusion.16
  (13 shorter events, 0.0 us)
Async XLA Ops:
  6.5 1.9 copy-start
  6.5 111.4 %reduce-scatter.2.cloned.1.call-start = ((), (), s32[]{:S(2)}) async-start(), calls=%async_computation.1 | async-start | bytes 11796480 | tf_op jit(solution)/shard_map/reduce_scatter | solution.py:20
  117.9 4.7 collective-permute-start
  122.6 1.4 copy-start.4
  170.4 46.2 %copy-start.2 = (bf16[768,1536]{1,0:T(8,128)(2,1)}, bf16[768,1536]{1,0:T(8,128)(2,1)S(1)}, u32[]{:S(2)}) copy-start(bf16[768,1536]{1,0:T(8,128)(2,1)S(1)} %fusion.2) | copy-start | bytes 7077892
  170.4 46.1 %collective-permute-start.1 = (bf16[768,1536]{1,0:T(8,128)(2,1)S(1)}, bf16[768,1536]{1,0:T(8,128)(2,1)S(1)}, u32[]{:S(2)}, u32[]{:S(2)}) collective-permute-start(bf16[768,1536]{1,0:T(8,128)(2,1)S(1)} %fusion.2), channel_id=1, source_target_pairs={{0,8},{4,12},{8,0},{12,4},{16,24},{20,28},{24,16},{28,20},{32,40},... | collective-permute-start | bytes 7077896 | tf_op jit(solution)/shard_map/ppermute | solution.py:10
  216.5 2.1 copy-start.5
  263.6 89.5 %copy-start.1 = (bf16[768,1536]{1,0:T(8,128)(2,1)}, bf16[768,1536]{1,0:T(8,128)(2,1)S(1)}, u32[]{:S(2)}) copy-start(bf16[768,1536]{1,0:T(8,128)(2,1)S(1)} %fusion.7) | copy-start | bytes 7077892
  263.6 89.4 %collective-permute-start.2 = (bf16[768,1536]{1,0:T(8,128)(2,1)S(1)}, bf16[768,1536]{1,0:T(8,128)(2,1)S(1)}, u32[]{:S(2)}, u32[]{:S(2)}) collective-permute-start(bf16[768,1536]{1,0:T(8,128)(2,1)S(1)} %fusion.7), channel_id=1, source_target_pairs={{0,16},{4,20},{8,24},{12,28},{16,0},{20,4},{24,8},{28,12},{32,48},... | collective-permute-start | bytes 7077896 | tf_op jit(solution)/shard_map/ppermute | solution.py:10
  353.0 2.0 copy-start.3
  400.5 101.3 %collective-permute-start.3 = (bf16[768,1536]{1,0:T(8,128)(2,1)}, bf16[768,1536]{1,0:T(8,128)(2,1)}, u32[]{:S(2)}, u32[]{:S(2)}) collective-permute-start(bf16[768,1536]{1,0:T(8,128)(2,1)} %get-tuple-element.30), channel_id=1, source_target_pairs={{0,32},{4,36},{8,40},{12,44},{16,48},{20,52},{24,56},{28,60},{32,0... | collective-permute-start | bytes 7077896 | tf_op jit(solution)/shard_map/ppermute | solution.py:10
Sparse Core Ops, SparseCore 0:
  23.5 94.3 reduce-scatter.1
where the time goes:
time: 558 us
  waiting for transfers between devices  326 us (58%)
  blocking collectives  151 us (27%)
  other arithmetic  28.8 us (5%)
  between operations  23.7 us (4%)
  matrix products  14.9 us (3%)
  starting transfers between devices  9.98 us (2%)
    ppermute x4, waiting for transfers between devices, from_partner(): lax.ppermute(array, axis, [(i, i ^ 1 << distance) for i in range(lax.axis...  232 us
    psum x4, blocking collectives, shards(): lax.psum((jnp.sum(first * second), jnp.sum(first * first), jnp.sum(second...  151 us
    reduce_scatter x1, waiting for transfers between devices, shards(): lax.psum_scatter(lax.dot_general(cotangent, context, (((0,), (0,)), ((),...  94.5 us
    dot_general x1, matrix products, shards(): lax.dot_general(cotangent, context, (((0,), (0,)), ((), ())), preferred_e...  14.9 us
    reduce_sum x4, other arithmetic, shards(): jnp.sum(first * first)  12.1 us
  transfers between devices with their start and end apart: 5, of which 5 were waited for; matrix products, arithmetic and copies ran while one was open for 0% of the time, Pallas kernels for 0%

commit v1 on v0

v1 whole, which is shorter than its diff:
```python
import functools
import jax
import jax.numpy as jnp
from jax import lax
from jax.experimental import pallas as pl
from jax.experimental.pallas import tpu as pltpu
from jax.sharding import PartitionSpec as P

EPS = 1e-06
MESH = pl.DeviceIdType.MESH
F32 = jnp.float32
BF16 = jnp.bfloat16


def xor_roll(x, distance, axis, index, size):
    up = pltpu.roll(x, x.shape[axis] - distance, axis)
    down = pltpu.roll(x, distance, axis)
    return jnp.where((index & distance) == 0, up, down)


def merge_weights(gram, n, levels):
    row = lax.broadcasted_iota(jnp.int32, gram.shape, 0)
    lane = lax.broadcasted_iota(jnp.int32, gram.shape, 1)
    diagonal = row == lane
    weights_t = jnp.where(diagonal, 1.0, 0.0).astype(F32)

    def mixing(aa, bb, ab):
        aa, bb = jnp.maximum(aa, 0.0), jnp.maximum(bb, 0.0)
        bound = jnp.sqrt(aa) * jnp.sqrt(bb)
        ab = jnp.clip(ab, -bound, bound)
        return 1.0 - ab / (2.0 * (aa + EPS)), 1.0 - ab / (2.0 * (bb + EPS))

    for level in range(levels):
        d = 1 << level
        partner = (row ^ d) == lane
        gram_r = xor_roll(gram, d, 0, row, n)
        gram_l = xor_roll(gram, d, 1, lane, n)

        def column(x, mask):
            return jnp.sum(jnp.where(mask, x, 0.0), axis=1, keepdims=True)

        def line(x, mask):
            return jnp.sum(jnp.where(mask, x, 0.0), axis=0, keepdims=True)

        ca, cb = mixing(column(gram, diagonal), column(gram_r, partner), column(gram, partner))
        ra, rb = mixing(line(gram, diagonal), line(gram_l, partner), line(gram, partner))
        mixed = ca * gram + cb * gram_r
        gram = ra * mixed + rb * xor_roll(mixed, d, 1, lane, n)
        weights_t = ra * weights_t + rb * xor_roll(weights_t, d, 1, lane, n)
    return weights_t[:, 0:1]


def kernel(ctx_hbm, cot_hbm, out_ref, ctx, cot, cot_t, p, xr, blocks, pairs, g1, g2,
           load_sem, xs_sem, xr_sem, as_sem, ar_sem, gs_sem, gr_sem):
    n_rack, n_outer, n_tp = lax.axis_size("rack"), lax.axis_size("outer"), lax.axis_size("tp")
    k, o, t = lax.axis_index("rack"), lax.axis_index("outer"), lax.axis_index("tp")
    left, right, opp = (k + 3) % 4, (k + 1) % 4, (k + 2) % 4
    z, core = o // 2, o % 2
    zh, zl = z // 4, z % 4
    tok, width = ctx.shape
    half = width // 2
    rack_rows = p.shape[0] // 4
    rows48 = rack_rows // 16
    step_rows = 2 * rows48
    unit_rows = rack_rows // 2
    dest = (opp, right, left, k)

    barrier = pltpu.get_barrier_semaphore()
    for d in range(1, n_rack * n_tp):
        dk, dt = d // n_tp, d % n_tp
        pl.semaphore_signal(
            barrier, inc=1,
            device_id={"rack": (k + dk) % n_rack, "tp": (t + dt) % n_tp}, device_id_type=MESH)
    for d in range(1, n_outer):
        pl.semaphore_signal(
            barrier, inc=1, device_id={"outer": (o + d) % n_outer}, device_id_type=MESH)

    def target(s):
        return (zh ^ (1 - s // 4)) * 4 + (zl + s + s // 4) % 4

    def source(s):
        return (zh ^ (1 - s // 4)) * 4 + (zl + 8 - s - s // 4) % 4

    def unit_cols(u):
        h = zh ^ (1 - u // 4)
        return dest[u % 4] * rack_rows + h * unit_rows

    def cot_load(u):
        cols = pl.ds(pl.multiple_of(unit_cols(u), 128), unit_rows)
        return pltpu.make_async_copy(cot_hbm.at[:, cols], cot.at[u], load_sem.at[u])

    ctx_load = pltpu.make_async_copy(ctx_hbm, ctx, load_sem.at[8])
    cot_load(0).start()
    ctx_load.start()
    for u in range(1, 8):
        cot_load(u).start()

    def unit(u):
        cot_load(u).wait()

        @pl.loop(0, 4)
        def _(r):
            part = pl.ds(pl.multiple_of(r * (tok // 4), tok // 4), tok // 4)
            cot_t[:, part] = cot[u, part, :].T

        base = pl.multiple_of(unit_cols(u), 128)
        tile = width // 6

        @pl.loop(0, 6)
        def _(i):
            cols = pl.ds(pl.multiple_of(i * tile, tile), tile)
            p[pl.ds(base, unit_rows), cols] = jnp.dot(
                cot_t[...], ctx[:, cols], preferred_element_type=F32).astype(BF16)

    side = (pl.ds(0, half), pl.ds(half, half))

    def rows_of(j, s):
        return pl.ds(pl.multiple_of(j * rack_rows + target(s) * step_rows, 16), step_rows)

    def message(kind, s):
        j, h, to = (
            (opp, 0, left), (right, 0, right), (opp, 1, right), (left, 1, left),
            (left, 0, left), (right, 1, right))[kind]
        return pltpu.make_async_remote_copy(
            src_ref=p.at[rows_of(j, s), side[h]],
            dst_ref=xr.at[s, kind],
            send_sem=xs_sem.at[s, kind],
            recv_sem=xr_sem.at[s, kind],
            device_id={"rack": to}, device_id_type=MESH)

    def add_into(rows, h, received):
        @pl.loop(0, step_rows // 16)
        def _(r):
            here = pl.ds(pl.multiple_of(rows.start + r * 16, 16), 16)
            there = pl.ds(pl.multiple_of(r * 16, 16), 16)
            total = p[here, side[h]].astype(F32)
            for s, kind in received:
                total = total + xr[s, kind, there, :].astype(F32)
            p[here, side[h]] = total.astype(BF16)

    def first_hops(s):
        for kind in (0, 2, 3, 1):
            message(kind, s).start()

    def relay(s):
        message(0, s).wait_recv()
        add_into(rows_of(left, s), 0, ((s, 0),))
        message(4, s).start()
        message(2, s).wait_recv()
        add_into(rows_of(right, s), 1, ((s, 2),))
        message(5, s).start()

    def block_send(s, c):
        to = target(s) * 2 + c
        start = k * rack_rows + target(s) * step_rows + c * rows48
        return pltpu.make_async_remote_copy(
            src_ref=p.at[pl.ds(pl.multiple_of(start, 16), rows48)],
            dst_ref=blocks.at[o],
            send_sem=as_sem.at[s, c],
            recv_sem=ar_sem.at[o],
            device_id={"outer": to}, device_id_type=MESH)

    def block_recv(q):
        return pltpu.make_async_remote_copy(
            src_ref=blocks.at[q], dst_ref=blocks.at[q], send_sem=as_sem.at[0, 0],
            recv_sem=ar_sem.at[q], device_id={"outer": q}, device_id_type=MESH)

    def peer_send():
        to = o ^ 1
        start = k * rack_rows + to * rows48
        return pltpu.make_async_remote_copy(
            src_ref=p.at[pl.ds(pl.multiple_of(start, 16), rows48)],
            dst_ref=blocks.at[o],
            send_sem=as_sem.at[7, 0],
            recv_sem=ar_sem.at[o],
            device_id={"outer": to}, device_id_type=MESH)

    def finish(s):
        rows = rows_of(k, s)
        message(1, s).wait_recv()
        message(4, s).wait_recv()
        add_into(rows, 0, ((s, 1), (s, 4)))
        message(3, s).wait_recv()
        message(5, s).wait_recv()
        add_into(rows, 1, ((s, 3), (s, 5)))
        if s < 7:
            for c in range(2):
                block_send(s, c).start()
        else:
            peer_send().start()
            start = k * rack_rows + o * rows48
            blocks[o] = p[pl.ds(pl.multiple_of(start, 16), rows48), :]

    def gram(s):
        q0 = source(s) * 2
        if s < 7:
            block_recv(q0).wait_recv()
            block_recv(q0 + 1).wait_recv()
        else:
            block_recv(o ^ 1).wait_recv()

        def older(m, carry):
            q = source(m // 2) * 2 + m % 2
            sums = [jnp.zeros((8, 128), F32), jnp.zeros((8, 128), F32)]
            for r in range(rows48 // 16):
                rows = pl.ds(r * 16, 16)
                for c in range(width // 128):
                    cols = pl.ds(c * 128, 128)
                    other = blocks[q, rows, cols].astype(F32)
                    for i in range(2):
                        product = blocks[q0 + i, rows, cols].astype(F32) * other
                        sums[i] = sums[i] + product[0:8] + product[8:16]
            for i in range(2):
                line = jnp.sum(sums[i], axis=0, keepdims=True)
                pairs[q0 + i, pl.ds(q, 1), :] = line
                pairs[q, pl.ds(q0 + i, 1), :] = line
            return carry

        lax.fori_loop(0, 2 * s + 2, older, 0)

    ctx_load.wait()
    unit(0)
    pl.semaphore_wait(barrier, n_rack * n_tp - 1 + n_outer - 1)
    for s in range(2):
        for kind in (0, 2):
            message(kind, s).start()
    unit(1)
    unit(2)
    for s in range(2):
        for kind in (3, 1):
            message(kind, s).start()
    unit(3)
    for s in range(8):
        relay(s)
        if s + 2 < 8:
            if s == 2:
                unit(5)
                unit(6)
            if s < 2:
                first_hops(s + 2)
                if s == 1:
                    unit(4)
            else:
                first_hops(s + 2)
        if s == 3:
            unit(7)
        if s >= 1:
            finish(s - 1)
        if s >= 4:
            gram(s - 4)
    for s in range(4, 7):
        gram(s)
    finish(7)
    gram(7)

    rowsum = jnp.sum(pairs[...], axis=2, keepdims=True)
    j_index = lax.broadcasted_iota(jnp.int32, (n_outer, n_outer, 128), 1)
    lanes = lax.broadcasted_iota(jnp.int32, (n_outer, n_outer, 128), 2)
    me1 = k * n_tp + t
    g1[me1] = jnp.sum(jnp.where(j_index == lanes, rowsum, 0.0), axis=1)

    def share1(d):
        to_k, to_t = (k + d // n_tp) % n_rack, (t + d % n_tp) % n_tp
        return pltpu.make_async_remote_copy(
            src_ref=g1.at[me1], dst_ref=g1.at[me1], send_sem=gs_sem.at[0, d],
            recv_sem=gr_sem.at[0, me1], device_id={"rack": to_k, "tp": to_t}, device_id_type=MESH)

    def share1_recv(d):
        from_k, from_t = (k + d // n_tp) % n_rack, (t + d % n_tp) % n_tp
        q = from_k * n_tp + from_t
        return pltpu.make_async_remote_copy(
            src_ref=g1.at[q], dst_ref=g1.at[q], send_sem=gs_sem.at[0, d],
            recv_sem=gr_sem.at[0, q], device_id={"rack": from_k, "tp": from_t}, device_id_type=MESH)

    for d in range(1, n_rack * n_tp):
        share1(d).start()
    for d in range(1, n_rack * n_tp):
        share1_recv(d).wait_recv()
    g2[o] = jnp.sum(g1[...], axis=0)

    def share2(d):
        return pltpu.make_async_remote_copy(
            src_ref=g2.at[o], dst_ref=g2.at[o], send_sem=gs_sem.at[1, d],
            recv_sem=gr_sem.at[1, o], device_id={"outer": (o + d) % n_outer}, device_id_type=MESH)

    def share2_recv(d):
        q = (o + d) % n_outer
        return pltpu.make_async_remote_copy(
            src_ref=g2.at[q], dst_ref=g2.at[q], send_sem=gs_sem.at[1, d],
            recv_sem=gr_sem.at[1, q], device_id={"outer": q}, device_id_type=MESH)

    for d in range(1, n_outer):
        share2(d).start()
    for d in range(1, n_outer):
        share2_recv(d).wait_recv()
    weights = merge_weights(jnp.sum(g2[...], axis=0), n_outer, 4)

    spread = [jnp.broadcast_to(weights[q:q + 1, 0:1], (16, 128)) for q in range(n_outer)]
    for r in range(rows48 // 16):
        for c in range(width // 128):
            at = (pl.ds(r * 16, 16), pl.ds(c * 128, 128))
            total = spread[0] * blocks[(0,) + at].astype(F32)
            for q in range(1, n_outer):
                total = total + spread[q] * blocks[(q,) + at].astype(F32)
            out_ref[at] = total.astype(BF16)

    for s in range(8):
        for kind in range(6):
            message(kind, s).wait_send()
        if s < 7:
            for c in range(2):
                block_send(s, c).wait_send()
    peer_send().wait_send()
    for d in range(1, n_rack * n_tp):
        share1(d).wait_send()
    for d in range(1, n_outer):
        share2(d).wait_send()


def shards(context, cotangent):
    tok, width = context.shape
    cols = cotangent.shape[1]
    n_outer = lax.axis_size("outer")
    rack_rows = cols // 4
    rows48 = rack_rows // 16
    return pl.pallas_call(
        kernel,
        out_shape=jax.ShapeDtypeStruct((rows48, width), BF16),
        in_specs=[pl.BlockSpec(memory_space=pl.ANY)] * 2,
        out_specs=pl.BlockSpec(memory_space=pltpu.VMEM),
        scratch_shapes=[
            pltpu.VMEM((tok, width), BF16),
            pltpu.VMEM((8, tok, rack_rows // 2), BF16),
            pltpu.VMEM((rack_rows // 2, tok), BF16),
            pltpu.VMEM((cols, width), BF16),
            pltpu.VMEM((8, 6, 2 * rows48, width // 2), BF16),
            pltpu.VMEM((n_outer, rows48, width), BF16),
            pltpu.VMEM((n_outer, n_outer, 128), F32),
            pltpu.VMEM((16, n_outer, 128), F32),
            pltpu.VMEM((16, n_outer, 128), F32),
            pltpu.SemaphoreType.DMA((9,)),
            pltpu.SemaphoreType.DMA((8, 6)),
            pltpu.SemaphoreType.DMA((8, 6)),
            pltpu.SemaphoreType.DMA((8, 2)),
            pltpu.SemaphoreType.DMA((16,)),
            pltpu.SemaphoreType.DMA((2, 16)),
            pltpu.SemaphoreType.DMA((2, 16)),
        ],
        compiler_params=pltpu.CompilerParams(
            collective_id=0, has_side_effects=True, vmem_limit_bytes=56 * 2**20),
    )(context, cotangent)


def solution(mesh):
    return jax.shard_map(
        shards,
        mesh=mesh,
        in_specs=(P(("rack", "outer"), "tp"), P(("rack", "outer"), None)),
        out_specs=P(("rack", "outer"), "tp"),
        check_vma=False,
    )
```

time: 558 us -> 124 us (0.22)
  the two profiles are of different devices: /device:TPU:8 before, /device:TPU:1 now
where the time goes in v1:
time: 124 us
  Pallas kernels  122 us (98%)
  local copies, waits for them, and re-layouts  1.58 us (1%)
    pallas_call x1, Pallas kernels, shards(): pl.pallas_call(kernel, out_shape=jax.ShapeDtypeStruct((rows48, width), BF...  122 us

profile of v1, /device:TPU:1, one launch (start us, length us, event | category | flops | bytes accessed | tf_op | source)
XLA Modules:
  0.0 123.9 jit_solution(9642151624826962751)
XLA Ops:
  0.0 122.3 %shard_map.28 = bf16[48,1536]{1,0:T(8,128)(2,1)} custom-call(bf16[1024,1536]{1,0:T(8,128)(2,1)} %ctx_hbm.1, bf16[1024,3072]{1,0:T(8,128)(2,1)} %cot_hbm.1), custom_call_target="tpu_custom_call" | custom-call | tf_op jit(solution)/shard_map/pallas_call | solution.py:326
  122.3 1.6 %copy.4 = bf16[48,1536]{1,0:T(8,128)(2,1)} copy(bf16[48,1536]{1,0:T(8,128)(2,1)} %shard_map.28) | data formatting | bytes 294912

commit v2 on v1

v2 whole, which is shorter than its diff:
```python
import functools
import jax
import jax.numpy as jnp
from jax import lax
from jax.experimental import pallas as pl
from jax.experimental.pallas import tpu as pltpu
from jax.sharding import PartitionSpec as P

EPS = 1e-06
MESH = pl.DeviceIdType.MESH
F32 = jnp.float32
BF16 = jnp.bfloat16


def xor_roll(x, distance, axis, index, size):
    up = pltpu.roll(x, x.shape[axis] - distance, axis)
    down = pltpu.roll(x, distance, axis)
    return jnp.where((index & distance) == 0, up, down)


def merge_weights(gram, n, levels):
    row = lax.broadcasted_iota(jnp.int32, gram.shape, 0)
    lane = lax.broadcasted_iota(jnp.int32, gram.shape, 1)
    diagonal = row == lane
    weights_t = jnp.where(diagonal, 1.0, 0.0).astype(F32)

    def mixing(aa, bb, ab):
        aa, bb = jnp.maximum(aa, 0.0), jnp.maximum(bb, 0.0)
        bound = jnp.sqrt(aa) * jnp.sqrt(bb)
        ab = jnp.clip(ab, -bound, bound)
        return 1.0 - ab / (2.0 * (aa + EPS)), 1.0 - ab / (2.0 * (bb + EPS))

    for level in range(levels):
        d = 1 << level
        partner = (row ^ d) == lane
        gram_r = xor_roll(gram, d, 0, row, n)
        gram_l = xor_roll(gram, d, 1, lane, n)

        def column(x, mask):
            return jnp.sum(jnp.where(mask, x, 0.0), axis=1, keepdims=True)

        def line(x, mask):
            return jnp.sum(jnp.where(mask, x, 0.0), axis=0, keepdims=True)

        ca, cb = mixing(column(gram, diagonal), column(gram_r, partner), column(gram, partner))
        ra, rb = mixing(line(gram, diagonal), line(gram_l, partner), line(gram, partner))
        mixed = ca * gram + cb * gram_r
        gram = ra * mixed + rb * xor_roll(mixed, d, 1, lane, n)
        weights_t = ra * weights_t + rb * xor_roll(weights_t, d, 1, lane, n)
    return weights_t[:, 0:1]


def kernel(ctx_hbm, cot_hbm, out_ref, ctx, cot, p, xr, blocks, pairs, g1, g2,
           load_sem, xs_sem, xr_sem, as_sem, ar_sem, gs_sem, gr_sem, near_sem, far_sem, core_sem):
    n_rack, n_outer, n_tp = lax.axis_size("rack"), lax.axis_size("outer"), lax.axis_size("tp")
    k, o, t = lax.axis_index("rack"), lax.axis_index("outer"), lax.axis_index("tp")
    left, right, opp = (k + 3) % 4, (k + 1) % 4, (k + 2) % 4
    z, core = o // 2, o % 2
    zh, zl = z // 4, z % 4
    tok, width = ctx.shape
    half = width // 2
    rack_rows = p.shape[0] // 4
    rows48 = rack_rows // 16
    step_rows = 2 * rows48
    unit_rows = rack_rows // 2
    dest = (opp, right, left, k)

    def along_z(d):
        return {"outer": (z + d) % 8 * 2 + core}

    adjacent = [{"rack": left}, {"rack": right}, {"tp": (t + 1) % 4}, {"tp": (t + 3) % 4},
                along_z(1), along_z(7)]
    second = [{"rack": left}, {"rack": right}, {"rack": opp}, along_z(2), along_z(6)]
    barrier = pltpu.get_barrier_semaphore()
    for device in adjacent + [{"outer": o ^ 1}]:
        pl.semaphore_signal(barrier, inc=1, device_id=device, device_id_type=MESH)

    def greet(semaphore, devices):
        for device in devices:
            pl.semaphore_signal(semaphore, inc=1, device_id=device, device_id_type=MESH)

    def target(s):
        h = s // 4
        return (zh ^ (1 - h)) * 4 + (zl ^ (s + h * (7 - 2 * s)))

    def unit_cols(u):
        h = zh ^ (1 - u // 4)
        return dest[u % 4] * rack_rows + h * unit_rows

    def cot_load(u):
        cols = pl.ds(pl.multiple_of(unit_cols(u), 128), unit_rows)
        return pltpu.make_async_copy(cot_hbm.at[:, cols], cot.at[u], load_sem.at[u])

    def ctx_load(h):
        cols = pl.ds(h * half, half)
        return pltpu.make_async_copy(ctx_hbm.at[:, cols], ctx.at[:, cols], load_sem.at[8 + h])

    cot_load(0).start()
    for h in range(2):
        ctx_load(h).start()
    for u in range(1, 8):
        cot_load(u).start()

    def product(u, h):
        cols = pl.ds(pl.multiple_of(h * half, half), half)
        p[pl.ds(pl.multiple_of(unit_cols(u), 128), unit_rows), cols] = lax.dot_general(
            cot[u], ctx[:, cols], (((0,), (0,)), ((), ())),
            preferred_element_type=F32).astype(BF16)

    def unit(u):
        cot_load(u).wait()

        @pl.loop(0, 2)
        def _(h):
            product(u, h)

    part = half // 3
    pieces = [(s, 0, half) for s in range(7)] + [(7, i * part, part) for i in range(3)]

    def side(h, i):
        _, first, size = pieces[i]
        return pl.ds(h * half + first, size)

    def rows_of(j, s):
        return pl.ds(pl.multiple_of(j * rack_rows + target(s) * step_rows, 16), step_rows)

    def message(kind, i):
        s, first, size = pieces[i]
        j, h, to = (
            (opp, 0, left), (right, 0, right), (opp, 1, right), (left, 1, left),
            (left, 0, left), (right, 1, right))[kind]
        return pltpu.make_async_remote_copy(
            src_ref=p.at[rows_of(j, s), side(h, i)],
            dst_ref=xr.at[s, kind, :, pl.ds(first, size)],
            send_sem=xs_sem.at[i, kind],
            recv_sem=xr_sem.at[i, kind],
            device_id={"rack": to}, device_id_type=MESH)

    def add_into(j, h, i, kinds):
        s, first, size = pieces[i]
        rows = rows_of(j, s)

        @pl.loop(0, step_rows // 16)
        def _(r):
            here = pl.ds(pl.multiple_of(rows.start + r * 16, 16), 16)
            there = pl.ds(pl.multiple_of(r * 16, 16), 16)
            total = p[here, side(h, i)].astype(F32)
            for kind in kinds:
                total = total + xr[s, kind, there, pl.ds(first, size)].astype(F32)
            p[here, side(h, i)] = total.astype(BF16)

    def first_hops(i):
        for kind in (0, 2, 3, 1):
            message(kind, i).start()

    def relay(i):
        message(0, i).wait_recv()
        add_into(left, 0, i, (0,))
        message(4, i).start()
        message(2, i).wait_recv()
        add_into(right, 1, i, (2,))
        message(5, i).start()

    def block_send(s, c):
        to = target(s) * 2 + c
        start = k * rack_rows + target(s) * step_rows + c * rows48
        return pltpu.make_async_remote_copy(
            src_ref=p.at[pl.ds(pl.multiple_of(start, 16), rows48)],
            dst_ref=blocks.at[o],
            send_sem=as_sem.at[s, c],
            recv_sem=ar_sem.at[o],
            device_id={"outer": to}, device_id_type=MESH)

    def block_recv(q):
        return pltpu.make_async_remote_copy(
            src_ref=blocks.at[q], dst_ref=blocks.at[q], send_sem=as_sem.at[0, 0],
            recv_sem=ar_sem.at[q], device_id={"outer": q}, device_id_type=MESH)

    def peer_copy(h, i, slot):
        start = k * rack_rows + (o ^ 1) * rows48
        return pltpu.make_async_remote_copy(
            src_ref=p.at[pl.ds(pl.multiple_of(start, 16), rows48), side(h, i)],
            dst_ref=blocks.at[slot, :, side(h, i)],
            send_sem=as_sem.at[i, h],
            recv_sem=ar_sem.at[n_outer + 2 * (i - 7) + h],
            device_id={"outer": o ^ 1}, device_id_type=MESH)

    def finish(i):
        s = pieces[i][0]
        for h, kinds in ((0, (1, 4)), (1, (3, 5))):
            for kind in kinds:
                message(kind, i).wait_recv()
            add_into(k, h, i, kinds)
            if s == 7:
                peer_copy(h, i, o).start()
        if s < 7:
            for c in range(2):
                block_send(s, c).start()
        else:
            start = pl.multiple_of(k * rack_rows + o * rows48, 16)
            for h in range(2):
                blocks[o, :, side(h, i)] = p[pl.ds(start, rows48), side(h, i)]

    def gram(i):
        s, first, size = pieces[i]
        q0 = target(s) * 2
        if s < 7:
            block_recv(q0).wait_recv()
            block_recv(q0 + 1).wait_recv()
        else:
            for h in range(2):
                peer_copy(h, i, o ^ 1).wait_recv()

        def inner(q, newer):
            sums = [jnp.zeros((8, 128), F32) for _ in newer]
            for r in range(rows48 // 16):
                rows = pl.ds(r * 16, 16)
                for c in range(2 * size // 128):
                    h, c = c // (size // 128), c % (size // 128)
                    cols = pl.ds(h * half + first + c * 128, 128)
                    other = blocks[q, rows, cols].astype(F32)
                    for n, a in enumerate(newer):
                        term = blocks[q0 + a, rows, cols].astype(F32) * other
                        sums[n] = sums[n] + term[0:8] + term[8:16]
            for n, a in enumerate(newer):
                line = jnp.sum(sums[n], axis=0, keepdims=True)
                if first > 0:
                    line = line + pairs[q0 + a, pl.ds(q, 1), :]
                pairs[q0 + a, pl.ds(q, 1), :] = line
                pairs[q, pl.ds(q0 + a, 1), :] = line

        @pl.loop(0, 2 * s + 1)
        def _(m):
            inner(target(m // 2) * 2 + m % 2, (0, 1))

        inner(q0 + 1, (1,))

    cot_load(0).wait()
    ctx_load(0).wait()
    product(0, 0)
    pl.semaphore_wait(barrier, 7)
    message(0, 0).start()
    message(0, 1).start()
    greet(near_sem, adjacent)
    ctx_load(1).wait()
    product(0, 1)
    message(2, 0).start()
    message(2, 1).start()
    unit(2)
    message(3, 0).start()
    unit(1)
    message(1, 0).start()
    pl.semaphore_wait(near_sem, 6)
    greet(far_sem, second)
    message(3, 1).start()
    message(1, 1).start()
    unit(3)
    pl.semaphore_wait(far_sem, 5)
    greet(core_sem, [{"outer": o ^ 1}])
    for s in range(7):
        relay(s)
        if s == 0:
            pl.semaphore_wait(core_sem, 1)
        if s + 2 < 7:
            if s == 2:
                unit(6)
                unit(5)
            first_hops(s + 2)
        if s == 6:
            for kinds in ((0, 2), (3, 1)):
                for i in (7, 8, 9):
                    for kind in kinds:
                        message(kind, i).start()
        if s == 1:
            unit(4)
        if s == 3:
            unit(7)
        if s >= 1:
            finish(s - 1)
        if s >= 3:
            gram(s - 3)
    finish(6)
    for i in (7, 8, 9):
        relay(i)
    gram(4)
    gram(5)
    finish(7)
    gram(6)
    finish(8)
    gram(7)
    finish(9)
    gram(8)
    gram(9)

    rowsum = jnp.sum(pairs[...], axis=2, keepdims=True)
    j_index = lax.broadcasted_iota(jnp.int32, (n_outer, n_outer, 128), 1)
    lanes = lax.broadcasted_iota(jnp.int32, (n_outer, n_outer, 128), 2)
    me1 = k * n_tp + t
    g1[me1] = jnp.sum(jnp.where(j_index == lanes, rowsum, 0.0), axis=1)

    def share1(d):
        to_k, to_t = (k + d // n_tp) % n_rack, (t + d % n_tp) % n_tp
        return pltpu.make_async_remote_copy(
            src_ref=g1.at[me1], dst_ref=g1.at[me1], send_sem=gs_sem.at[0, d],
            recv_sem=gr_sem.at[0, me1], device_id={"rack": to_k, "tp": to_t}, device_id_type=MESH)

    def share1_recv(d):
        from_k, from_t = (k + d // n_tp) % n_rack, (t + d % n_tp) % n_tp
        q = from_k * n_tp + from_t
        return pltpu.make_async_remote_copy(
            src_ref=g1.at[q], dst_ref=g1.at[q], send_sem=gs_sem.at[0, d],
            recv_sem=gr_sem.at[0, q], device_id={"rack": from_k, "tp": from_t}, device_id_type=MESH)

    for d in range(1, n_rack * n_tp):
        share1(d).start()
    for i in range(10):
        for kind in range(6):
            message(kind, i).wait_send()
        for h in range(2):
            if i < 7:
                block_send(i, h).wait_send()
            else:
                peer_copy(h, i, o).wait_send()
    for d in range(1, n_rack * n_tp):
        share1_recv(d).wait_recv()
    g2[o] = jnp.sum(g1[...], axis=0)

    def share2(d):
        return pltpu.make_async_remote_copy(
            src_ref=g2.at[o], dst_ref=g2.at[o], send_sem=gs_sem.at[1, d],
            recv_sem=gr_sem.at[1, o], device_id={"outer": (o + d) % n_outer}, device_id_type=MESH)

    def share2_recv(d):
        q = (o + d) % n_outer
        return pltpu.make_async_remote_copy(
            src_ref=g2.at[q], dst_ref=g2.at[q], send_sem=gs_sem.at[1, d],
            recv_sem=gr_sem.at[1, q], device_id={"outer": q}, device_id_type=MESH)

    for d in range(1, n_outer):
        share2(d).start()
    for d in range(1, n_outer):
        share2_recv(d).wait_recv()
    weights = merge_weights(jnp.sum(g2[...], axis=0), n_outer, 4)

    spread = [jnp.broadcast_to(weights[q:q + 1, 0:1], (16, 128)) for q in range(n_outer)]
    for r in range(rows48 // 16):
        for c in range(width // 128):
            at = (pl.ds(r * 16, 16), pl.ds(c * 128, 128))
            total = spread[0] * blocks[(0,) + at].astype(F32)
            for q in range(1, n_outer):
                total = total + spread[q] * blocks[(q,) + at].astype(F32)
            out_ref[at] = total.astype(BF16)

    for d in range(1, n_rack * n_tp):
        share1(d).wait_send()
    for d in range(1, n_outer):
        share2(d).wait_send()


def shards(context, cotangent):
    tok, width = context.shape
    cols = cotangent.shape[1]
    n_outer = lax.axis_size("outer")
    rack_rows = cols // 4
    rows48 = rack_rows // 16
    return pl.pallas_call(
        kernel,
        out_shape=jax.ShapeDtypeStruct((rows48, width), BF16),
        in_specs=[pl.BlockSpec(memory_space=pl.ANY)] * 2,
        out_specs=pl.BlockSpec(memory_space=pltpu.VMEM),
        scratch_shapes=[
            pltpu.VMEM((tok, width), BF16),
            pltpu.VMEM((8, tok, rack_rows // 2), BF16),
            pltpu.VMEM((cols, width), BF16),
            pltpu.VMEM((8, 6, 2 * rows48, width // 2), BF16),
            pltpu.VMEM((n_outer, rows48, width), BF16),
            pltpu.VMEM((n_outer, n_outer, 128), F32),
            pltpu.VMEM((16, n_outer, 128), F32),
            pltpu.VMEM((16, n_outer, 128), F32),
            pltpu.SemaphoreType.DMA((10,)),
            pltpu.SemaphoreType.DMA((10, 6)),
            pltpu.SemaphoreType.DMA((10, 6)),
            pltpu.SemaphoreType.DMA((10, 2)),
            pltpu.SemaphoreType.DMA((22,)),
            pltpu.SemaphoreType.DMA((2, 16)),
            pltpu.SemaphoreType.DMA((2, 16)),
            pltpu.SemaphoreType.REGULAR,
            pltpu.SemaphoreType.REGULAR,
            pltpu.SemaphoreType.REGULAR,
        ],
        compiler_params=pltpu.CompilerParams(
            collective_id=0, has_side_effects=True, vmem_limit_bytes=56 * 2**20),
    )(context, cotangent)


def solution(mesh):
    return jax.shard_map(
        shards,
        mesh=mesh,
        in_specs=(P(("rack", "outer"), "tp"), P(("rack", "outer"), None)),
        out_specs=P(("rack", "outer"), "tp"),
        check_vma=False,
    )
```

time: 124 us -> 118 us (0.952)
  Pallas kernels: 122 us -> 116 us
    pallas_call x1, Pallas kernels: 122 us -> 116 us  [shards(): pl.pallas_call(kernel, out_shape=jax.ShapeDtypeStruct((rows48, width), BF...]
where the time goes in v2:
time: 118 us
  Pallas kernels  116 us (98%)
  local copies, waits for them, and re-layouts  1.58 us (1%)
    pallas_call x1, Pallas kernels, shards(): pl.pallas_call(kernel, out_shape=jax.ShapeDtypeStruct((rows48, width), BF...  116 us

profile of v2, /device:TPU:1, one launch (start us, length us, event | category | flops | bytes accessed | tf_op | source)
XLA Modules:
  0.0 117.6 jit_solution(7281424743272009758)
XLA Ops:
  0.0 116.0 %shard_map.28 = bf16[48,1536]{1,0:T(8,128)(2,1)} custom-call(bf16[1024,1536]{1,0:T(8,128)(2,1)} %ctx_hbm.1, bf16[1024,3072]{1,0:T(8,128)(2,1)} %cot_hbm.1), custom_call_target="tpu_custom_call" | custom-call | tf_op jit(solution)/shard_map/pallas_call | solution.py:366
  116.0 1.6 %copy.4 = bf16[48,1536]{1,0:T(8,128)(2,1)} copy(bf16[48,1536]{1,0:T(8,128)(2,1)} %shard_map.28) | data formatting | bytes 294912

commit v3 on v2

--- a/solution.py
+++ b/solution.py
@@ -79,9 +79,15 @@
         for device in devices:
             pl.semaphore_signal(semaphore, inc=1, device_id=device, device_id_type=MESH)
 
+    def distance(s):
+        odd = s % 2
+        return (1 - odd) * (4 + s // 2) + odd * ((7 - s) // 2)
+
     def target(s):
-        h = s // 4
-        return (zh ^ (1 - h)) * 4 + (zl ^ (s + h * (7 - 2 * s)))
+        return (z + distance(s)) % 8
+
+    def source(s):
+        return (z + 8 - distance(s)) % 8
 
     def unit_cols(u):
         h = zh ^ (1 - u // 4)
@@ -203,7 +209,7 @@
 
     def gram(i):
         s, first, size = pieces[i]
-        q0 = target(s) * 2
+        q0 = source(s) * 2
         if s < 7:
             block_recv(q0).wait_recv()
             block_recv(q0 + 1).wait_recv()
@@ -231,7 +237,7 @@
 
         @pl.loop(0, 2 * s + 1)
         def _(m):
-            inner(target(m // 2) * 2 + m % 2, (0, 1))
+            inner(source(m // 2) * 2 + m % 2, (0, 1))
 
         inner(q0 + 1, (1,))
 
@@ -240,43 +246,40 @@
     product(0, 0)
     pl.semaphore_wait(barrier, 7)
     message(0, 0).start()
-    message(0, 1).start()
     greet(near_sem, adjacent)
     ctx_load(1).wait()
     product(0, 1)
     message(2, 0).start()
-    message(2, 1).start()
     unit(2)
     message(3, 0).start()
     unit(1)
     message(1, 0).start()
     pl.semaphore_wait(near_sem, 6)
     greet(far_sem, second)
+    unit(4)
+    message(0, 1).start()
+    message(2, 1).start()
+    relay(0)
+    unit(6)
     message(3, 1).start()
+    unit(5)
     message(1, 1).start()
-    unit(3)
     pl.semaphore_wait(far_sem, 5)
     greet(core_sem, [{"outer": o ^ 1}])
-    for s in range(7):
+    first_hops(2)
+    unit(3)
+    unit(7)
+    pl.semaphore_wait(core_sem, 1)
+    for s in range(1, 7):
         relay(s)
-        if s == 0:
-            pl.semaphore_wait(core_sem, 1)
         if s + 2 < 7:
-            if s == 2:
-                unit(6)
-                unit(5)
             first_hops(s + 2)
         if s == 6:
             for kinds in ((0, 2), (3, 1)):
                 for i in (7, 8, 9):
                     for kind in kinds:
                         message(kind, i).start()
-        if s == 1:
-            unit(4)
-        if s == 3:
-            unit(7)
-        if s >= 1:
-            finish(s - 1)
+        finish(s - 1)
         if s >= 3:
             gram(s - 3)
     finish(6)

time: 118 us -> 109 us (0.924)
  Pallas kernels: 116 us -> 107 us
    pallas_call x1, Pallas kernels: 116 us -> 107 us  [shards(): pl.pallas_call(kernel, out_shape=jax.ShapeDtypeStruct((rows48, width), BF...]
where the time goes in v3:
time: 109 us
  Pallas kernels  107 us (98%)
  local copies, waits for them, and re-layouts  1.58 us (1%)
    pallas_call x1, Pallas kernels, shards(): pl.pallas_call(kernel, out_shape=jax.ShapeDtypeStruct((rows48, width), BF...  107 us

profile of v3, /device:TPU:1, one launch (start us, length us, event | category | flops | bytes accessed | tf_op | source)
XLA Modules:
  0.0 108.9 jit_solution(10967213527253507215)
XLA Ops:
  0.0 107.3 %shard_map.28 = bf16[48,1536]{1,0:T(8,128)(2,1)} custom-call(bf16[1024,1536]{1,0:T(8,128)(2,1)} %ctx_hbm.1, bf16[1024,3072]{1,0:T(8,128)(2,1)} %cot_hbm.1), custom_call_target="tpu_custom_call" | custom-call | tf_op jit(solution)/shard_map/pallas_call | solution.py:369
  107.3 1.6 %copy.4 = bf16[48,1536]{1,0:T(8,128)(2,1)} copy(bf16[48,1536]{1,0:T(8,128)(2,1)} %shard_map.28) | data formatting | bytes 294912

commit v4 on v3

--- a/solution.py
+++ b/solution.py
@@ -50,8 +50,9 @@
     return weights_t[:, 0:1]
 
 
-def kernel(ctx_hbm, cot_hbm, out_ref, ctx, cot, p, xr, blocks, pairs, g1, g2,
-           load_sem, xs_sem, xr_sem, as_sem, ar_sem, gs_sem, gr_sem, near_sem, far_sem, core_sem):
+def kernel(ctx_hbm, cot_hbm, out_hbm, out, ctx, cot, p, xr, blocks, pairs, lines, merged, g1, g2,
+           load_sem, xs_sem, xr_sem, as_sem, ar_sem, gs_sem, gr_sem, near_sem, far_sem, core_sem,
+           out_sem):
     n_rack, n_outer, n_tp = lax.axis_size("rack"), lax.axis_size("outer"), lax.axis_size("tp")
     k, o, t = lax.axis_index("rack"), lax.axis_index("outer"), lax.axis_index("tp")
     left, right, opp = (k + 3) % 4, (k + 1) % 4, (k + 2) % 4
@@ -120,8 +121,10 @@
         def _(h):
             product(u, h)
 
-    part = half // 3
-    pieces = [(s, 0, half) for s in range(7)] + [(7, i * part, part) for i in range(3)]
+    lane_tiles = half // 128
+    cuts = (0, lane_tiles // 2 * 128, lane_tiles * 5 // 6 * 128, half)
+    pieces = [(s, 0, half) for s in range(7)]
+    pieces += [(7, cuts[i], cuts[i + 1] - cuts[i]) for i in range(3)]
 
     def side(h, i):
         _, first, size = pieces[i]
@@ -167,26 +170,32 @@
         add_into(right, 1, i, (2,))
         message(5, i).start()
 
+    def slot(m):
+        return pl.ds(pl.multiple_of(m * rows48, 16), rows48)
+
+    def owner(m):
+        return source(m // 2) * 2 + m % 2
+
     def block_send(s, c):
         to = target(s) * 2 + c
         start = k * rack_rows + target(s) * step_rows + c * rows48
         return pltpu.make_async_remote_copy(
             src_ref=p.at[pl.ds(pl.multiple_of(start, 16), rows48)],
-            dst_ref=blocks.at[o],
+            dst_ref=blocks.at[slot(2 * s + core)],
             send_sem=as_sem.at[s, c],
-            recv_sem=ar_sem.at[o],
+            recv_sem=ar_sem.at[2 * s + core],
             device_id={"outer": to}, device_id_type=MESH)
 
-    def block_recv(q):
-        return pltpu.make_async_remote_copy(
-            src_ref=blocks.at[q], dst_ref=blocks.at[q], send_sem=as_sem.at[0, 0],
-            recv_sem=ar_sem.at[q], device_id={"outer": q}, device_id_type=MESH)
-
-    def peer_copy(h, i, slot):
+    def block_recv(m):
+        return pltpu.make_async_remote_copy(
+            src_ref=blocks.at[slot(m)], dst_ref=blocks.at[slot(m)], send_sem=as_sem.at[0, 0],
+            recv_sem=ar_sem.at[m], device_id={"outer": owner(m)}, device_id_type=MESH)
+
+    def peer_copy(h, i, m):
         start = k * rack_rows + (o ^ 1) * rows48
         return pltpu.make_async_remote_copy(
             src_ref=p.at[pl.ds(pl.multiple_of(start, 16), rows48), side(h, i)],
-            dst_ref=blocks.at[slot, :, side(h, i)],
+            dst_ref=blocks.at[slot(m), side(h, i)],
             send_sem=as_sem.at[i, h],
             recv_sem=ar_sem.at[n_outer + 2 * (i - 7) + h],
             device_id={"outer": o ^ 1}, device_id_type=MESH)
@@ -198,48 +207,49 @@
                 message(kind, i).wait_recv()
             add_into(k, h, i, kinds)
             if s == 7:
-                peer_copy(h, i, o).start()
+                peer_copy(h, i, 14 + core).start()
         if s < 7:
             for c in range(2):
                 block_send(s, c).start()
         else:
             start = pl.multiple_of(k * rack_rows + o * rows48, 16)
             for h in range(2):
-                blocks[o, :, side(h, i)] = p[pl.ds(start, rows48), side(h, i)]
+                blocks[slot(14 + core), side(h, i)] = p[pl.ds(start, rows48), side(h, i)]
 
     def gram(i):
         s, first, size = pieces[i]
-        q0 = source(s) * 2
         if s < 7:
-            block_recv(q0).wait_recv()
-            block_recv(q0 + 1).wait_recv()
+            for c in range(2):
+                block_recv(2 * s + c).wait_recv()
         else:
             for h in range(2):
-                peer_copy(h, i, o ^ 1).wait_recv()
-
-        def inner(q, newer):
-            sums = [jnp.zeros((8, 128), F32) for _ in newer]
-            for r in range(rows48 // 16):
-                rows = pl.ds(r * 16, 16)
-                for c in range(2 * size // 128):
-                    h, c = c // (size // 128), c % (size // 128)
-                    cols = pl.ds(h * half + first + c * 128, 128)
-                    other = blocks[q, rows, cols].astype(F32)
-                    for n, a in enumerate(newer):
-                        term = blocks[q0 + a, rows, cols].astype(F32) * other
-                        sums[n] = sums[n] + term[0:8] + term[8:16]
-            for n, a in enumerate(newer):
-                line = jnp.sum(sums[n], axis=0, keepdims=True)
-                if first > 0:
-                    line = line + pairs[q0 + a, pl.ds(q, 1), :]
-                pairs[q0 + a, pl.ds(q, 1), :] = line
-                pairs[q, pl.ds(q0 + a, 1), :] = line
-
-        @pl.loop(0, 2 * s + 1)
-        def _(m):
-            inner(source(m // 2) * 2 + m % 2, (0, 1))
-
-        inner(q0 + 1, (1,))
+                peer_copy(h, i, 15 - core).wait_recv()
+        count = 2 * s + 2
+        newest = pl.ds(2 * s * rows48, step_rows)
+        columns = (pl.ds(0, width),) if s < 7 else (side(0, i), side(1, i))
+        products = 0.0
+        for cols in columns:
+            products = products + lax.dot_general(
+                blocks[pl.ds(0, count * rows48), cols], blocks[newest, cols],
+                (((1,), (1,)), ((), ())), preferred_element_type=F32)
+        row = lax.broadcasted_iota(jnp.int32, (count, rows48, step_rows), 1)
+        lane = lax.broadcasted_iota(jnp.int32, (count, rows48, step_rows), 2)
+        mask = (row == lane) | (row + rows48 == lane)
+        trace = jnp.sum(
+            jnp.where(mask, products.reshape(count, rows48, step_rows), 0.0), axis=1)
+        if first > 0:
+            trace = trace + lines[...]
+        if s == 7 and i < 9:
+            lines[...] = trace
+            return
+        lane = lax.broadcasted_iota(jnp.int32, (count, step_rows), 1)
+        for a in range(2):
+            new = owner(2 * s + a)
+            mine = jnp.where(lane // rows48 == a, trace, 0.0)
+            for m in range(count):
+                pairs[new, pl.ds(owner(m), 1), :] = mine[m:m + 1]
+                if m < 2 * s:
+                    pairs[owner(m), pl.ds(new, 1), :] = mine[m:m + 1]
 
     cot_load(0).wait()
     ctx_load(0).wait()
@@ -290,8 +300,8 @@
     finish(7)
     gram(6)
     finish(8)
+    finish(9)
     gram(7)
-    finish(9)
     gram(8)
     gram(9)
 
@@ -314,7 +324,10 @@
             src_ref=g1.at[q], dst_ref=g1.at[q], send_sem=gs_sem.at[0, d],
             recv_sem=gr_sem.at[0, q], device_id={"rack": from_k, "tp": from_t}, device_id_type=MESH)
 
-    for d in range(1, n_rack * n_tp):
+    def hops(d):
+        return min(d // n_tp, n_rack - d // n_tp) + min(d % n_tp, n_tp - d % n_tp)
+
+    for d in sorted(range(1, n_rack * n_tp), key=hops, reverse=True):
         share1(d).start()
     for i in range(10):
         for kind in range(6):
@@ -323,7 +336,7 @@
             if i < 7:
                 block_send(i, h).wait_send()
             else:
-                peer_copy(h, i, o).wait_send()
+                peer_copy(h, i, 14 + core).wait_send()
     for d in range(1, n_rack * n_tp):
         share1_recv(d).wait_recv()
     g2[o] = jnp.sum(g1[...], axis=0)
@@ -339,20 +352,31 @@
             src_ref=g2.at[q], dst_ref=g2.at[q], send_sem=gs_sem.at[1, d],
             recv_sem=gr_sem.at[1, q], device_id={"outer": q}, device_id_type=MESH)
 
-    for d in range(1, n_outer):
+    for d in sorted(range(1, n_outer), key=lambda d: abs(2 * d - n_outer)):
         share2(d).start()
     for d in range(1, n_outer):
         share2_recv(d).wait_recv()
     weights = merge_weights(jnp.sum(g2[...], axis=0), n_outer, 4)
 
-    spread = [jnp.broadcast_to(weights[q:q + 1, 0:1], (16, 128)) for q in range(n_outer)]
+    merged[...] = jnp.broadcast_to(weights, merged.shape)
+    spread = [
+        jnp.broadcast_to(merged[pl.ds(owner(m), 1), :], (16, 128)) for m in range(n_outer)]
+
+    def out_copy(r):
+        rows = pl.ds(r * 16, 16)
+        return pltpu.make_async_copy(out.at[rows], out_hbm.at[rows], out_sem.at[r])
+
     for r in range(rows48 // 16):
         for c in range(width // 128):
-            at = (pl.ds(r * 16, 16), pl.ds(c * 128, 128))
-            total = spread[0] * blocks[(0,) + at].astype(F32)
-            for q in range(1, n_outer):
-                total = total + spread[q] * blocks[(q,) + at].astype(F32)
-            out_ref[at] = total.astype(BF16)
+            cols = pl.ds(c * 128, 128)
+            total = 0.0
+            for m in range(n_outer):
+                rows = pl.ds(m * rows48 + r * 16, 16)
+                total = total + spread[m] * blocks[rows, cols].astype(F32)
+            out[pl.ds(r * 16, 16), cols] = total.astype(BF16)
+        out_copy(r).start()
+    for r in range(rows48 // 16):
+        out_copy(r).wait()
 
     for d in range(1, n_rack * n_tp):
         share1(d).wait_send()
@@ -370,14 +394,17 @@
         kernel,
         out_shape=jax.ShapeDtypeStruct((rows48, width), BF16),
         in_specs=[pl.BlockSpec(memory_space=pl.ANY)] * 2,
-        out_specs=pl.BlockSpec(memory_space=pltpu.VMEM),
+        out_specs=pl.BlockSpec(memory_space=pl.ANY),
         scratch_shapes=[
+            pltpu.VMEM((rows48, width), BF16),
             pltpu.VMEM((tok, width), BF16),
             pltpu.VMEM((8, tok, rack_rows // 2), BF16),
             pltpu.VMEM((cols, width), BF16),
             pltpu.VMEM((8, 6, 2 * rows48, width // 2), BF16),
-            pltpu.VMEM((n_outer, rows48, width), BF16),
-            pltpu.VMEM((n_outer, n_outer, 128), F32),
+            pltpu.VMEM((n_outer * rows48, width), BF16),
+            pltpu.VMEM((n_outer, n_outer, 2 * rows48), F32),
+            pltpu.VMEM((n_outer, 2 * rows48), F32),
+            pltpu.VMEM((n_outer, 128), F32),
             pltpu.VMEM((16, n_outer, 128), F32),
             pltpu.VMEM((16, n_outer, 128), F32),
             pltpu.SemaphoreType.DMA((10,)),
@@ -390,6 +417,7 @@
             pltpu.SemaphoreType.REGULAR,
             pltpu.SemaphoreType.REGULAR,
             pltpu.SemaphoreType.REGULAR,
+            pltpu.SemaphoreType.DMA((rows48 // 16,)),
         ],
         compiler_params=pltpu.CompilerParams(
             collective_id=0, has_side_effects=True, vmem_limit_bytes=56 * 2**20),

time: 109 us -> 107 us (0.982)
  Pallas kernels: 107 us -> 105 us
    pallas_call x1, Pallas kernels: 107 us -> 105 us  [shards(): pl.pallas_call(kernel, out_shape=jax.ShapeDtypeStruct((rows48, width), BF...]
where the time goes in v4:
time: 107 us
  Pallas kernels  105 us (98%)
  local copies, waits for them, and re-layouts  1.58 us (1%)
    pallas_call x1, Pallas kernels, shards(): pl.pallas_call(kernel, out_shape=jax.ShapeDtypeStruct((rows48, width), BF...  105 us

profile of v4, /device:TPU:1, one launch (start us, length us, event | category | flops | bytes accessed | tf_op | source)
XLA Modules:
  0.0 106.9 jit_solution(4685997411766408661)
XLA Ops:
  0.0 105.3 %shard_map.28 = bf16[48,1536]{1,0:T(8,128)(2,1)} custom-call(bf16[1024,1536]{1,0:T(8,128)(2,1)} %ctx_hbm.1, bf16[1024,3072]{1,0:T(8,128)(2,1)} %cot_hbm.1), custom_call_target="tpu_custom_call" | custom-call | tf_op jit(solution)/shard_map/pallas_call | solution.py:393
  105.3 1.6 %copy.4 = bf16[48,1536]{1,0:T(8,128)(2,1)} copy(bf16[48,1536]{1,0:T(8,128)(2,1)} %shard_map.28) | data formatting | bytes 294912

commit v5 on v4

--- a/solution.py
+++ b/solution.py
@@ -50,9 +50,9 @@
     return weights_t[:, 0:1]
 
 
-def kernel(ctx_hbm, cot_hbm, out_hbm, out, ctx, cot, p, xr, blocks, pairs, lines, merged, g1, g2,
+def kernel(ctx_hbm, cot_hbm, out_hbm, out, ctx, cot, p, xr, xq, blocks, pairs, lines, merged, g1, g2,
            load_sem, xs_sem, xr_sem, as_sem, ar_sem, gs_sem, gr_sem, near_sem, far_sem, core_sem,
-           out_sem):
+           out_sem, ps_sem, pr_sem, os_sem, or_sem):
     n_rack, n_outer, n_tp = lax.axis_size("rack"), lax.axis_size("outer"), lax.axis_size("tp")
     k, o, t = lax.axis_index("rack"), lax.axis_index("outer"), lax.axis_index("tp")
     left, right, opp = (k + 3) % 4, (k + 1) % 4, (k + 2) % 4
@@ -108,8 +108,9 @@
     for u in range(1, 8):
         cot_load(u).start()
 
-    def product(u, h):
-        cols = pl.ds(pl.multiple_of(h * half, half), half)
+    def product(u, h, parts=1, part=0):
+        size = half // parts
+        cols = pl.ds(pl.multiple_of(h * half + part * size, size), size)
         p[pl.ds(pl.multiple_of(unit_cols(u), 128), unit_rows), cols] = lax.dot_general(
             cot[u], ctx[:, cols], (((0,), (0,)), ((), ())),
             preferred_element_type=F32).astype(BF16)
@@ -132,18 +133,33 @@
 
     def rows_of(j, s):
         return pl.ds(pl.multiple_of(j * rack_rows + target(s) * step_rows, 16), step_rows)
+
+    def rows_for(j, group):
+        return pl.ds(pl.multiple_of(j * rack_rows + group * rows48, 16), rows48)
 
     def message(kind, i):
         s, first, size = pieces[i]
         j, h, to = (
             (opp, 0, left), (right, 0, right), (opp, 1, right), (left, 1, left),
             (left, 0, left), (right, 1, right))[kind]
-        return pltpu.make_async_remote_copy(
-            src_ref=p.at[rows_of(j, s), side(h, i)],
-            dst_ref=xr.at[s, kind, :, pl.ds(first, size)],
+        rows, there = rows_of(j, s), pl.ds(0, step_rows)
+        if i == 9 and kind >= 4:
+            rows, there = rows_for(j, o), pl.ds(pl.multiple_of(core * rows48, 16), rows48)
+        return pltpu.make_async_remote_copy(
+            src_ref=p.at[rows, side(h, i)],
+            dst_ref=xr.at[s, kind, there, pl.ds(first, size)],
             send_sem=xs_sem.at[i, kind],
             recv_sem=xr_sem.at[i, kind],
             device_id={"rack": to}, device_id_type=MESH)
+
+    def passed(h):
+        j = (left, right)[h]
+        return pltpu.make_async_remote_copy(
+            src_ref=p.at[rows_for(j, o ^ 1), side(h, 9)],
+            dst_ref=xq.at[h],
+            send_sem=ps_sem.at[h],
+            recv_sem=pr_sem.at[h],
+            device_id={"rack": j, "outer": o ^ 1}, device_id_type=MESH)
 
     def add_into(j, h, i, kinds):
         s, first, size = pieces[i]
@@ -158,17 +174,37 @@
                 total = total + xr[s, kind, there, pl.ds(first, size)].astype(F32)
             p[here, side(h, i)] = total.astype(BF16)
 
+    def opening(h, c):
+        cols = pl.ds(c * (half // 2), half // 2)
+        return pltpu.make_async_remote_copy(
+            src_ref=p.at[rows_of(opp, 0), pl.ds(h * half + c * (half // 2), half // 2)],
+            dst_ref=xr.at[0, 2 * h, :, cols],
+            send_sem=os_sem.at[h, c],
+            recv_sem=or_sem.at[h, c],
+            device_id={"rack": (left, right)[h]}, device_id_type=MESH)
+
+    def arrived(h, i):
+        if i == 0:
+            for c in range(2):
+                opening(h, c).wait_recv()
+        else:
+            message(2 * h, i).wait_recv()
+
     def first_hops(i):
         for kind in (0, 2, 3, 1):
             message(kind, i).start()
 
     def relay(i):
-        message(0, i).wait_recv()
+        arrived(0, i)
         add_into(left, 0, i, (0,))
         message(4, i).start()
-        message(2, i).wait_recv()
+        if i == 9:
+            passed(0).start()
+        arrived(1, i)
         add_into(right, 1, i, (2,))
         message(5, i).start()
+        if i == 9:
+            passed(1).start()
 
     def slot(m):
         return pl.ds(pl.multiple_of(m * rows48, 16), rows48)
@@ -216,17 +252,44 @@
             for h in range(2):
                 blocks[slot(14 + core), side(h, i)] = p[pl.ds(start, rows48), side(h, i)]
 
+    def finish_last():
+        first, size = pieces[9][1:]
+        cols = pl.ds(first, size)
+        mine = pl.ds(pl.multiple_of(core * rows48, 16), rows48)
+        theirs = pl.ds(pl.multiple_of((1 - core) * rows48, 16), rows48)
+        for h, kind in ((0, 1), (1, 3)):
+            message(kind, 9).wait_recv()
+            rows = rows_for(k, o ^ 1)
+            total = p[rows, side(h, 9)].astype(F32) + xr[7, kind, theirs, cols].astype(F32)
+            p[rows, side(h, 9)] = total.astype(BF16)
+            peer_copy(h, 9, 14 + core).start()
+        for h, kind in ((0, 1), (1, 3)):
+            message(kind // 2 + 4, 9).wait_recv()
+            total = p[rows_for(k, o), side(h, 9)].astype(F32)
+            for part in (kind, kind // 2 + 4):
+                total = total + xr[7, part, mine, cols].astype(F32)
+            blocks[slot(14 + core), side(h, 9)] = total.astype(BF16)
+
     def gram(i):
-        s, first, size = pieces[i]
+        s, first = pieces[i][:2]
         if s < 7:
             for c in range(2):
                 block_recv(2 * s + c).wait_recv()
         else:
             for h in range(2):
-                peer_copy(h, i, 15 - core).wait_recv()
+                for part in ((7,) if i == 7 else (8, 9)):
+                    peer_copy(h, part, 15 - core).wait_recv()
+                if i == 8:
+                    passed(h).wait_recv()
+                    here = slot(15 - core)
+                    total = blocks[here, side(h, 9)].astype(F32) + xq[h].astype(F32)
+                    blocks[here, side(h, 9)] = total.astype(BF16)
         count = 2 * s + 2
         newest = pl.ds(2 * s * rows48, step_rows)
-        columns = (pl.ds(0, width),) if s < 7 else (side(0, i), side(1, i))
+        columns = (pl.ds(0, width),)
+        if s == 7:
+            size = cuts[1] if i == 7 else half - cuts[1]
+            columns = tuple(pl.ds(h * half + first, size) for h in range(2))
         products = 0.0
         for cols in columns:
             products = products + lax.dot_general(
@@ -239,7 +302,7 @@
             jnp.where(mask, products.reshape(count, rows48, step_rows), 0.0), axis=1)
         if first > 0:
             trace = trace + lines[...]
-        if s == 7 and i < 9:
+        if i == 7:
             lines[...] = trace
             return
         lane = lax.broadcasted_iota(jnp.int32, (count, step_rows), 1)
@@ -253,27 +316,41 @@
 
     cot_load(0).wait()
     ctx_load(0).wait()
-    product(0, 0)
+    product(0, 0, 2, 0)
     pl.semaphore_wait(barrier, 7)
-    message(0, 0).start()
+    opening(0, 0).start()
+    ctx_load(1).wait()
+    product(0, 1, 2, 0)
+    opening(1, 0).start()
+    product(0, 0, 2, 1)
+    opening(0, 1).start()
+    product(0, 1, 2, 1)
+    opening(1, 1).start()
     greet(near_sem, adjacent)
-    ctx_load(1).wait()
-    product(0, 1)
-    message(2, 0).start()
-    unit(2)
+    cot_load(2).wait()
+    product(2, 1)
     message(3, 0).start()
-    unit(1)
+    cot_load(1).wait()
+    product(1, 0)
     message(1, 0).start()
     pl.semaphore_wait(near_sem, 6)
     greet(far_sem, second)
-    unit(4)
+    cot_load(4).wait()
+    product(4, 0)
     message(0, 1).start()
+    product(4, 1)
     message(2, 1).start()
+    product(2, 0)
+    product(1, 1)
     relay(0)
-    unit(6)
+    cot_load(6).wait()
+    product(6, 1)
     message(3, 1).start()
-    unit(5)
+    cot_load(5).wait()
+    product(5, 0)
     message(1, 1).start()
+    product(6, 0)
+    product(5, 1)
     pl.semaphore_wait(far_sem, 5)
     greet(core_sem, [{"outer": o ^ 1}])
     first_hops(2)
@@ -300,10 +377,9 @@
     finish(7)
     gram(6)
     finish(8)
-    finish(9)
+    finish_last()
     gram(7)
     gram(8)
-    gram(9)
 
     rowsum = jnp.sum(pairs[...], axis=2, keepdims=True)
     j_index = lax.broadcasted_iota(jnp.int32, (n_outer, n_outer, 128), 1)
@@ -331,12 +407,18 @@
         share1(d).start()
     for i in range(10):
         for kind in range(6):
-            message(kind, i).wait_send()
+            if i == 0 and kind in (0, 2):
+                for c in range(2):
+                    opening(kind // 2, c).wait_send()
+            else:
+                message(kind, i).wait_send()
         for h in range(2):
             if i < 7:
                 block_send(i, h).wait_send()
             else:
                 peer_copy(h, i, 14 + core).wait_send()
+    for h in range(2):
+        passed(h).wait_send()
     for d in range(1, n_rack * n_tp):
         share1_recv(d).wait_recv()
     g2[o] = jnp.sum(g1[...], axis=0)
@@ -401,6 +483,7 @@
             pltpu.VMEM((8, tok, rack_rows // 2), BF16),
             pltpu.VMEM((cols, width), BF16),
             pltpu.VMEM((8, 6, 2 * rows48, width // 2), BF16),
+            pltpu.VMEM((2, rows48, width // 12), BF16),
             pltpu.VMEM((n_outer * rows48, width), BF16),
             pltpu.VMEM((n_outer, n_outer, 2 * rows48), F32),
             pltpu.VMEM((n_outer, 2 * rows48), F32),
@@ -418,6 +501,10 @@
             pltpu.SemaphoreType.REGULAR,
             pltpu.SemaphoreType.REGULAR,
             pltpu.SemaphoreType.DMA((rows48 // 16,)),
+            pltpu.SemaphoreType.DMA((2,)),
+            pltpu.SemaphoreType.DMA((2,)),
+            pltpu.SemaphoreType.DMA((2, 2)),
+            pltpu.SemaphoreType.DMA((2, 2)),
         ],
         compiler_params=pltpu.CompilerParams(
             collective_id=0, has_side_effects=True, vmem_limit_bytes=56 * 2**20),

time: 107 us -> 106 us (level)
  no operation moved by 1% of the time
where the time goes in v5:
time: 106 us
  Pallas kernels  105 us (99%)
  local copies, waits for them, and re-layouts  1.58 us (1%)
    pallas_call x1, Pallas kernels, shards(): pl.pallas_call(kernel, out_shape=jax.ShapeDtypeStruct((rows48, width), BF...  105 us

profile of v5, /device:TPU:1, one launch (start us, length us, event | category | flops | bytes accessed | tf_op | source)
XLA Modules:
  0.0 106.1 jit_solution(16388654587761956317)
XLA Ops:
  0.0 104.5 %shard_map.28 = bf16[48,1536]{1,0:T(8,128)(2,1)} custom-call(bf16[1024,1536]{1,0:T(8,128)(2,1)} %ctx_hbm.1, bf16[1024,3072]{1,0:T(8,128)(2,1)} %cot_hbm.1), custom_call_target="tpu_custom_call" | custom-call | tf_op jit(solution)/shard_map/pallas_call | solution.py:475
  104.5 1.6 %copy.4 = bf16[48,1536]{1,0:T(8,128)(2,1)} copy(bf16[48,1536]{1,0:T(8,128)(2,1)} %shard_map.28) | data formatting | bytes 294912

commit v6 on v5

--- a/solution.py
+++ b/solution.py
@@ -370,9 +370,10 @@
         if s >= 3:
             gram(s - 3)
     finish(6)
-    for i in (7, 8, 9):
-        relay(i)
+    relay(7)
     gram(4)
+    relay(8)
+    relay(9)
     gram(5)
     finish(7)
     gram(6)

time: 106 us -> 106 us (level)
  no operation moved by 1% of the time
where the time goes in v6:
time: 106 us
  Pallas kernels  105 us (99%)
  local copies, waits for them, and re-layouts  1.58 us (1%)
    pallas_call x1, Pallas kernels, shards(): pl.pallas_call(kernel, out_shape=jax.ShapeDtypeStruct((rows48, width), BF...  105 us

profile of v6, /device:TPU:1, one launch (start us, length us, event | category | flops | bytes accessed | tf_op | source)
XLA Modules:
  0.0 106.1 jit_solution(5872758680088487585)
XLA Ops:
  0.0 104.5 %shard_map.28 = bf16[48,1536]{1,0:T(8,128)(2,1)} custom-call(bf16[1024,1536]{1,0:T(8,128)(2,1)} %ctx_hbm.1, bf16[1024,3072]{1,0:T(8,128)(2,1)} %cot_hbm.1), custom_call_target="tpu_custom_call" | custom-call | tf_op jit(solution)/shard_map/pallas_call | solution.py:476
  104.5 1.6 %copy.4 = bf16[48,1536]{1,0:T(8,128)(2,1)} copy(bf16[48,1536]{1,0:T(8,128)(2,1)} %shard_map.28) | data formatting | bytes 294912

commit v7 on v6

--- a/solution.py
+++ b/solution.py
@@ -374,8 +374,8 @@
     gram(4)
     relay(8)
     relay(9)
+    finish(7)
     gram(5)
-    finish(7)
     gram(6)
     finish(8)
     finish_last()

time: 106 us -> 107 us (level)
    pallas_call x1, Pallas kernels: 105 us -> 106 us  [shards(): pl.pallas_call(kernel, out_shape=jax.ShapeDtypeStruct((rows48, width), BF...]
where the time goes in v7:
time: 107 us
  Pallas kernels  106 us (99%)
  local copies, waits for them, and re-layouts  1.58 us (1%)
    pallas_call x1, Pallas kernels, shards(): pl.pallas_call(kernel, out_shape=jax.ShapeDtypeStruct((rows48, width), BF...  106 us

profile of v7, /device:TPU:1, one launch (start us, length us, event | category | flops | bytes accessed | tf_op | source)
XLA Modules:
  0.0 107.2 jit_solution(1261047083249676729)
XLA Ops:
  0.0 105.6 %shard_map.28 = bf16[48,1536]{1,0:T(8,128)(2,1)} custom-call(bf16[1024,1536]{1,0:T(8,128)(2,1)} %ctx_hbm.1, bf16[1024,3072]{1,0:T(8,128)(2,1)} %cot_hbm.1), custom_call_target="tpu_custom_call" | custom-call | tf_op jit(solution)/shard_map/pallas_call | solution.py:476
  105.6 1.6 %copy.4 = bf16[48,1536]{1,0:T(8,128)(2,1)} copy(bf16[48,1536]{1,0:T(8,128)(2,1)} %shard_map.28) | data formatting | bytes 294912
